TPU v7x, 256 devices: a whole 4x4x8 slice. The times are simulated.
256 devices in a mesh: dp: 64 (over x_lo, y, z), rep: 4 (over x_hi, core).
Axes of the slice: x: 4 (x_hi: 2, x_lo: 2; x = x_hi * 2 + x_lo), y: 4, z: 8, core: 2. Of those that a mesh axis runs over, the one named last changes fastest.
Arguments:
- picture_embeds: bfloat16 [196608, 1152], P(('dp', 'rep')), may hold values from -0.1875 to 0.1875
- caption_embeds: bfloat16 [196608, 1152], P(('dp', 'rep')), may hold values from -0.1875 to 0.1875
- sharpness_multiplier: float32 [1], replicated, may hold values from 4 to 16
- offset_shift: float32 [1], replicated, may hold values from -4 to -1
Outputs:
- photo_entry_costs: float32 [196608], P(('dp', 'rep'))
- photo_adjoint: float32 [196608, 1152], P(('dp', 'rep'))
- sentence_adjoint: float32 [196608, 1152], P(('dp', 'rep'))
All inputs are finite; a program needn't handle non-finite values.
Results may differ from a plain program's by a relative error of at most 0.0025.
Values may be sent and summed in bfloat16 or wider, within the bound.
A program may use at most 64 MiB of HBM per device.

v0:
```python
import jax
import jax.numpy as jnp
from jax import lax
from jax.sharding import PartitionSpec as P

STEPS = 2


def from_behind(value, axis, steps):
    count = lax.axis_size(axis)
    pairs = [(source, (source + steps) % count) for source in range(count)]
    return lax.ppermute(value, axis, pairs)


def matched_shares(
    picture_slab, caption_slab, sharpness_multiplier, offset_shift, resident_caption
):
    similarity_table = (
        sharpness_multiplier[0]
        * jnp.dot(picture_slab, caption_slab.T, preferred_element_type=jnp.float32)
        + offset_shift[0]
    )
    if resident_caption:
        positive = jnp.eye(picture_slab.shape[0], dtype=jnp.float32)
    else:
        positive = jnp.zeros((picture_slab.shape[0], picture_slab.shape[0]), jnp.float32)
    sign = 2.0 * positive - 1.0
    loss = jnp.sum(-jax.nn.log_sigmoid(sign * similarity_table), axis=1)
    target_plus_minus = (jax.nn.sigmoid(similarity_table) - positive).astype(jnp.bfloat16)
    return (loss, target_plus_minus)


def shards(picture_embeds, caption_embeds, sharpness_multiplier, offset_shift):
    odds_multiplier = sharpness_multiplier[0]
    photo_entry_costs, target_plus_minus = matched_shares(
        picture_embeds, caption_embeds, sharpness_multiplier, offset_shift, True
    )
    photo_adjoint = odds_multiplier * jnp.dot(
        target_plus_minus, caption_embeds, preferred_element_type=jnp.float32
    )
    sentence_adjoint = odds_multiplier * jnp.dot(
        target_plus_minus.T, picture_embeds, preferred_element_type=jnp.float32
    )
    arriving_caption = caption_embeds
    carried = sentence_adjoint
    for circulation_round in range(STEPS):
        arriving_caption = from_behind(arriving_caption, ("dp", "rep"), 1)
        carried = from_behind(carried, ("dp", "rep"), 1)
        running_cost_total, target_plus_minus = matched_shares(
            picture_embeds, arriving_caption, sharpness_multiplier, offset_shift, False
        )
        photo_entry_costs = photo_entry_costs + running_cost_total
        photo_adjoint = photo_adjoint + odds_multiplier * jnp.dot(
            target_plus_minus, arriving_caption, preferred_element_type=jnp.float32
        )
        carried = carried + odds_multiplier * jnp.dot(
            target_plus_minus.T, picture_embeds, preferred_element_type=jnp.float32
        )
    sentence_adjoint = from_behind(carried, ("dp", "rep"), -STEPS)
    return (photo_entry_costs, photo_adjoint, sentence_adjoint)


def solution(mesh):
    in_specs = (P(("dp", "rep"), None), P(("dp", "rep"), None), P(), P())
    out_specs = (P(("dp", "rep")), P(("dp", "rep"), None), P(("dp", "rep"), None))
    return jax.shard_map(shards, mesh=mesh, in_specs=in_specs, out_specs=out_specs, check_vma=False)
```

profile of v0, /device:TPU:1, one launch (start us, length us, event | category | flops | bytes accessed | tf_op | source)
XLA Modules:
  0.0 229.2 jit_solution(13729487115199511274)
XLA Ops:
  0.6 0.0 copy-start
  2.1 0.1 copy-done
  2.1 4.3 %fusion.2 = (f32[768]{0:T(1024)S(1)}, f32[768,768]{0,1:T(8,128)S(1)}) fusion(f32[]{:T(128)} %bitcast.23, f32[]{:T(128)} %bitcast.14, bf16[768,1152]{1,0:T(8,128)(2,1)S(1)} %copy-done, bf16[768,1152]{1,0:T(8,128)(2,1)} %param.5), kind=kOutput, calls=%fused_computation.10 | convolution fusion | flops 1367211264 | bytes 5901320 | tf_op jit(solution)/shard_map/dot_general | solution.py:20
  6.4 0.0 copy-start.1
  6.4 2.0 convolution_multiply_fusion.2
  8.5 4.2 %collective-permute-start.2 = (f32[768,1152]{1,0:T(8,128)S(1)}, f32[768,1152]{1,0:T(8,128)S(1)}, u32[]{:S(2)}, u32[]{:S(2)}) collective-permute-start(f32[768,1152]{1,0:T(8,128)S(1)} %convolution_multiply_fusion.2), channel_id=1, source_target_pairs={{0,1},{1,2},{2,3},{3,4},{4,5},{5,6},{6,7},{7,8},{8,9},{9,10},{10,1... | collective-permute-start | bytes 10616840 | tf_op jit(solution)/shard_map/ppermute | solution.py:12
  12.7 0.0 copy-done.1
  12.7 0.1 collective-permute-start
  12.8 57.3 %collective-permute-done = bf16[768,1152]{1,0:T(8,128)(2,1)S(1)} collective-permute-done((bf16[768,1152]{1,0:T(8,128)(2,1)S(1)}, bf16[768,1152]{1,0:T(8,128)(2,1)S(1)}, u32[]{:S(2)}, u32[]{:S(2)}) %collective-permute-start) | collective-permute-done | bytes 1769504 | tf_op jit(solution)/shard_map/ppermute | solution.py:12
  70.1 2.7 %fusion.3 = (f32[768]{0:T(1024)S(1)}, f32[768,768]{0,1:T(8,128)S(1)}) fusion(f32[]{:T(128)} %bitcast.28, f32[]{:T(128)} %bitcast.19, bf16[768,1152]{1,0:T(8,128)(2,1)S(1)} %copy-done, bf16[768,1152]{1,0:T(8,128)(2,1)S(1)} %collective-permute-done), kind=kOutput, calls=%fused_computation.11 | convolution fusion | flops 1365441792 | bytes 5901320 | tf_op jit(solution)/shard_map/dot_general | solution.py:20
  72.8 0.0 collective-permute-done.2
  72.8 2.1 fusion
  74.9 4.1 %collective-permute-start.3 = (f32[768,1152]{1,0:T(8,128)S(1)}, f32[768,1152]{1,0:T(8,128)S(1)}, u32[]{:S(2)}, u32[]{:S(2)}) collective-permute-start(f32[768,1152]{1,0:T(8,128)S(1)} %fusion), channel_id=1, source_target_pairs={{0,1},{1,2},{2,3},{3,4},{4,5},{5,6},{6,7},{7,8},{8,9},{9,10},{10,1... | collective-permute-start | bytes 10616840 | tf_op jit(solution)/shard_map/ppermute | solution.py:12
  79.0 0.3 collective-permute-start.1
  79.2 57.1 %collective-permute-done.1 = bf16[768,1152]{1,0:T(8,128)(2,1)S(1)} collective-permute-done((bf16[768,1152]{1,0:T(8,128)(2,1)S(1)}, bf16[768,1152]{1,0:T(8,128)(2,1)S(1)}, u32[]{:S(2)}, u32[]{:S(2)}) %collective-permute-start.1) | collective-permute-done | bytes 1769504 | tf_op jit(solution)/shard_map/ppermute | solution.py:12
  136.4 2.7 %fusion.4 = (f32[768]{0:T(1024)S(1)}, f32[768,768]{0,1:T(8,128)S(1)}) fusion(f32[]{:T(128)} %bitcast.27, f32[]{:T(128)} %bitcast.22, bf16[768,1152]{1,0:T(8,128)(2,1)S(1)} %copy-done, bf16[768,1152]{1,0:T(8,128)(2,1)S(1)} %collective-permute-done.1), kind=kOutput, calls=%fused_computation.12 | convolution fusion | flops 1365441792 | bytes 5901320 | tf_op jit(solution)/shard_map/dot_general | solution.py:20
  139.1 2.0 convolution_multiply_fusion
  141.1 0.0 collective-permute-done.3
  141.1 0.4 add.68
  141.5 10.9 %collective-permute-start.4 = (f32[768,1152]{1,0:T(8,128)S(1)}, f32[768,1152]{1,0:T(8,128)S(1)}, u32[]{:S(2)}, u32[]{:S(2)}) collective-permute-start(f32[768,1152]{1,0:T(8,128)S(1)} %add.68), channel_id=1, source_target_pairs={{0,254},{1,255},{2,0},{3,1},{4,2},{5,3},{6,4},{7,5},{8,6},{9,7},{1... | collective-permute-start | bytes 10616840 | tf_op jit(solution)/shard_map/ppermute | solution.py:12
  152.4 1.8 fusion.5
  154.3 1.9 convolution_add_fusion.1
  156.2 0.6 add_add_fusion
  156.8 3.7 %fusion.1 = f32[768,1152]{1,0:T(8,128)} fusion(f32[768,1152]{1,0:T(8,128)S(1)} %convolution_add_fusion.1, bf16[768,1152]{1,0:T(8,128)(2,1)S(1)} %collective-permute-done.1, f32[]{:T(128)} %bitcast.15, f32[768,768]{0,1:T(8,128)S(1)} %get-tuple-element.4, f32[]{:T(128)} %bitcast.24), kind=kOutput, calls=%fused_computation.8 | convolution fusion | flops 1364262912 | bytes 11206664 | tf_op jit(solution)/shard_map/dot_general | solution.py:53
  160.6 66.9 %collective-permute-done.4 = f32[768,1152]{1,0:T(8,128)S(1)} collective-permute-done((f32[768,1152]{1,0:T(8,128)S(1)}, f32[768,1152]{1,0:T(8,128)S(1)}, u32[]{:S(2)}, u32[]{:S(2)}) %collective-permute-start.4) | collective-permute-done | bytes 3538976 | tf_op jit(solution)/shard_map/ppermute | solution.py:12
  227.4 1.8 copy.10
Async XLA Ops:
  0.6 1.5 copy-start
  6.4 6.3 %copy-start.1 = (bf16[768,1152]{1,0:T(8,128)(2,1)S(1)}, bf16[768,1152]{1,0:T(8,128)(2,1)}, u32[]{:S(2)}) copy-start(bf16[768,1152]{1,0:T(8,128)(2,1)} %param.5) | copy-start | bytes 5308420
  8.5 64.3 %collective-permute-start.2 = (f32[768,1152]{1,0:T(8,128)S(1)}, f32[768,1152]{1,0:T(8,128)S(1)}, u32[]{:S(2)}, u32[]{:S(2)}) collective-permute-start(f32[768,1152]{1,0:T(8,128)S(1)} %convolution_multiply_fusion.2), channel_id=1, source_target_pairs={{0,1},{1,2},{2,3},{3,4},{4,5},{5,6},{6,7},{7,8},{8,9},{9,10},{10,1... | collective-permute-start | bytes 10616840 | tf_op jit(solution)/shard_map/ppermute | solution.py:12
  12.7 57.4 %collective-permute-start = (bf16[768,1152]{1,0:T(8,128)(2,1)S(1)}, bf16[768,1152]{1,0:T(8,128)(2,1)S(1)}, u32[]{:S(2)}, u32[]{:S(2)}) collective-permute-start(bf16[768,1152]{1,0:T(8,128)(2,1)S(1)} %copy-done.1), channel_id=1, source_target_pairs={{0,1},{1,2},{2,3},{3,4},{4,5},{5,6},{6,7},{7,8},{8,9},{9,10},{10,1... | collective-permute-start | bytes 5308424 | tf_op jit(solution)/shard_map/ppermute | solution.py:12
  74.9 66.2 %collective-permute-start.3 = (f32[768,1152]{1,0:T(8,128)S(1)}, f32[768,1152]{1,0:T(8,128)S(1)}, u32[]{:S(2)}, u32[]{:S(2)}) collective-permute-start(f32[768,1152]{1,0:T(8,128)S(1)} %fusion), channel_id=1, source_target_pairs={{0,1},{1,2},{2,3},{3,4},{4,5},{5,6},{6,7},{7,8},{8,9},{9,10},{10,1... | collective-permute-start | bytes 10616840 | tf_op jit(solution)/shard_map/ppermute | solution.py:12
  79.0 57.4 %collective-permute-start.1 = (bf16[768,1152]{1,0:T(8,128)(2,1)S(1)}, bf16[768,1152]{1,0:T(8,128)(2,1)S(1)}, u32[]{:S(2)}, u32[]{:S(2)}) collective-permute-start(bf16[768,1152]{1,0:T(8,128)(2,1)S(1)} %collective-permute-done), channel_id=1, source_target_pairs={{0,1},{1,2},{2,3},{3,4},{4,5},{5,6},{6,7},{7,8},{8,9},{9,10},{10,1... | collective-permute-start | bytes 5308424 | tf_op jit(solution)/shard_map/ppermute | solution.py:12
  141.5 85.9 %collective-permute-start.4 = (f32[768,1152]{1,0:T(8,128)S(1)}, f32[768,1152]{1,0:T(8,128)S(1)}, u32[]{:S(2)}, u32[]{:S(2)}) collective-permute-start(f32[768,1152]{1,0:T(8,128)S(1)} %add.68), channel_id=1, source_target_pairs={{0,254},{1,255},{2,0},{3,1},{4,2},{5,3},{6,4},{7,5},{8,6},{9,7},{1... | collective-permute-start | bytes 10616840 | tf_op jit(solution)/shard_map/ppermute | solution.py:12
where the time goes:
time: 229 us
  waiting for transfers between devices  181 us (79%)
  matrix products  23.4 us (10%)
  starting transfers between devices  19.6 us (9%)
    ppermute x5, waiting for transfers between devices, from_behind(): return lax.ppermute(value, axis, pairs)  181 us
    ppermute x5, starting transfers between devices, from_behind(): return lax.ppermute(value, axis, pairs)  19.6 us
    dot_general x3, matrix products, matched_shares(): jnp.dot(picture_slab, caption_slab.T, preferred_element_type=jnp.float32)  9.77 us
    dot_general x3, matrix products, shards(): jnp.dot(target_plus_minus.T, picture_embeds, preferred_element_type=jnp.f...  6.13 us
    dot_general x2, matrix products, shards(): jnp.dot(target_plus_minus, arriving_caption, preferred_element_type=jnp.f...  5.68 us
  transfers between devices with their start and end apart: 5, of which 3 were waited for; matrix products, arithmetic and copies ran while one was open for 7% of the time, Pallas kernels for 0%

commit v1 on v0

v1 whole, which is shorter than its diff:
```python
import jax
import jax.numpy as jnp
from jax import lax
from jax.experimental import pallas as pl
from jax.experimental.pallas import tpu as pltpu
from jax.sharding import PartitionSpec as P

MESH = pl.DeviceIdType.MESH
N_REP = 4
DEVICES = 256
ROWS = 768
WIDTH = 1152
CHUNK = 128
CHUNKS = ROWS // CHUNK
TILE = 256
LATE_WINDOW = 3
EARLY_WINDOW = 2


def kernel(
    scale_ref, shift_ref, text_ref, image_ref,
    loss_out, image_out, text_out,
    own, got_far, got_near, beside, passed, grads, losses,
    load_sem, store_sem, far_send, far_recv, near_send, near_recv, pass_send, pass_recv, beside_sem,
):
    dp, rep = lax.axis_index("dp"), lax.axis_index("rep")
    parity = lax.rem(rep, 2)
    me = dp * N_REP + rep

    def place(index):
        index = lax.rem(index + DEVICES, DEVICES)
        return (index // N_REP, lax.rem(index, N_REP))

    far_target = place(me - 2 + 4 * parity)
    near_target = place(me + 2 - 4 * parity)
    partner = (dp, rep + 1 - 2 * parity)

    loads = [
        pltpu.make_async_copy(text_ref, own.at[parity], load_sem.at[0]),
        pltpu.make_async_copy(image_ref, own.at[1 - parity], load_sem.at[1]),
    ]
    for load in loads:
        load.start()
    barrier = pltpu.get_barrier_semaphore()
    for target in (far_target, near_target, partner):
        pl.semaphore_signal(barrier, inc=1, device_id=target, device_id_type=MESH)

    scale = scale_ref[0]
    shift = shift_ref[0]

    def rows(chunk):
        return pl.ds(pl.multiple_of(chunk * CHUNK, CHUNK), CHUNK)

    def far_copy(chunk):
        return pltpu.make_async_remote_copy(
            src_ref=own.at[1, rows(chunk)], dst_ref=got_far.at[rows(chunk)],
            send_sem=far_send.at[chunk], recv_sem=far_recv.at[chunk],
            device_id=far_target, device_id_type=MESH,
        )

    def near_copy(chunk):
        return pltpu.make_async_remote_copy(
            src_ref=own.at[0, rows(chunk)], dst_ref=got_near.at[rows(chunk)],
            send_sem=near_send.at[chunk], recv_sem=near_recv.at[chunk],
            device_id=near_target, device_id_type=MESH,
        )

    def pass_copy(chunk):
        return pltpu.make_async_remote_copy(
            src_ref=got_far.at[rows(chunk)], dst_ref=passed.at[rows(chunk)],
            send_sem=pass_send.at[chunk], recv_sem=pass_recv.at[chunk],
            device_id=partner, device_id_type=MESH,
        )

    beside_copy = pltpu.make_async_remote_copy(
        src_ref=own.at[0], dst_ref=beside, send_sem=beside_sem.at[0], recv_sem=beside_sem.at[1],
        device_id=partner, device_id_type=MESH,
    )

    def meet(slot, other, start, count, diagonal, finish=None):
        block = other[pl.ds(start, count), :]
        for tile in range(ROWS // TILE):
            part = pl.ds(tile * TILE, TILE)
            logits = (
                lax.dot_general(
                    own[slot, part, :], block, (((1,), (1,)), ((), ())), preferred_element_type=jnp.float32
                )
                * scale
                + shift
            )
            decay = jnp.exp(-jnp.abs(logits))
            chance = jnp.where(logits >= 0, 1.0, decay) / (1.0 + decay)
            if diagonal:
                row = lax.broadcasted_iota(jnp.int32, (TILE, count), 0) + tile * TILE
                column = lax.broadcasted_iota(jnp.int32, (TILE, count), 1) + start
                same = row == column
                coef = chance - jnp.where(same, 1.0, 0.0)
                against = jnp.where(same, -logits, logits)
            else:
                coef = chance
                against = logits
            cost = jnp.maximum(against, 0.0) + jnp.log1p(decay)
            total = cost[:, :128]
            for piece in range(1, count // 128):
                total = total + cost[:, piece * 128 : (piece + 1) * 128]
            losses[slot, part, :] += total
            change = jnp.dot(coef.astype(jnp.bfloat16), block, preferred_element_type=jnp.float32)
            if finish is None:
                grads[slot, part, :] += change
            else:
                grads[slot, part, :] = (grads[slot, part, :] + change) * scale
                finish(tile)

    grads[...] = jnp.zeros_like(grads)
    losses[...] = jnp.zeros_like(losses)
    for load in loads:
        load.wait()
    pl.semaphore_wait(barrier, 3)

    far_copy(0).start()
    near_copy(0).start()
    beside_copy.start()
    for chunk in range(1, LATE_WINDOW):
        far_copy(chunk).start()
        if chunk < EARLY_WINDOW:
            near_copy(chunk).start()

    def local(step, carry):
        start = pl.multiple_of(step * TILE, TILE)
        meet(0, own.at[1], start, TILE, True)
        meet(1, own.at[0], start, TILE, True)
        return carry

    lax.fori_loop(0, ROWS // TILE, local, 0)
    beside_copy.wait()

    def inside(step, carry):
        meet(0, beside, pl.multiple_of(step * TILE, TILE), TILE, False)
        return carry

    lax.fori_loop(0, ROWS // TILE, inside, 0)

    def take_far(chunk):
        copy = far_copy(chunk)
        copy.wait_recv()
        pass_copy(chunk).start()
        copy.wait_send()

        @pl.when(chunk + LATE_WINDOW < CHUNKS)
        def _():
            far_copy(chunk + LATE_WINDOW).start()

        meet(0, got_far, pl.multiple_of(chunk * CHUNK, CHUNK), CHUNK, False)

    def take_passed(chunk):
        pass_copy(chunk).wait()
        meet(1, passed, pl.multiple_of(chunk * CHUNK, CHUNK), CHUNK, False)

    def take_near(chunk):
        copy = near_copy(chunk)
        copy.wait_recv()
        copy.wait_send()

        @pl.when(chunk + EARLY_WINDOW < CHUNKS)
        def _():
            near_copy(chunk + EARLY_WINDOW).start()

        meet(1, got_near, pl.multiple_of(chunk * CHUNK, CHUNK), CHUNK, False)

    take_far(0)

    def across(chunk, carry):
        take_far(chunk)
        take_passed(chunk - 1)
        take_near(chunk - 1)
        return carry

    lax.fori_loop(1, CHUNKS, across, 0)

    grads[0] = grads[0] * scale

    def near_store(output):
        return pltpu.make_async_copy(grads.at[0], output, store_sem.at[ROWS // TILE])

    def far_store(output, tile):
        part = pl.ds(tile * TILE, TILE)
        return pltpu.make_async_copy(grads.at[1, part], output.at[part], store_sem.at[tile])

    @pl.when(parity == 0)
    def _():
        near_store(text_out).start()

    @pl.when(parity == 1)
    def _():
        near_store(image_out).start()

    take_passed(CHUNKS - 1)
    last = near_copy(CHUNKS - 1)
    last.wait_recv()
    last.wait_send()

    def finish(tile):
        @pl.when(parity == 0)
        def _():
            far_store(image_out, tile).start()

        @pl.when(parity == 1)
        def _():
            far_store(text_out, tile).start()

    meet(1, got_near, ROWS - CHUNK, CHUNK, False, finish)
    loss_out[...] = jnp.sum(losses[1 - parity].T, axis=0, keepdims=True)
    near_store(text_out).wait()
    for tile in range(ROWS // TILE):
        far_store(image_out, tile).wait()


def shards(picture_embeds, caption_embeds, sharpness_multiplier, offset_shift):
    smem = pl.BlockSpec(memory_space=pltpu.SMEM)
    hbm = pl.BlockSpec(memory_space=pl.ANY)
    block = pltpu.VMEM((ROWS, WIDTH), jnp.bfloat16)
    loss, image, text = pl.pallas_call(
        kernel,
        out_shape=[
            jax.ShapeDtypeStruct((1, ROWS), jnp.float32),
            jax.ShapeDtypeStruct((ROWS, WIDTH), jnp.float32),
            jax.ShapeDtypeStruct((ROWS, WIDTH), jnp.float32),
        ],
        in_specs=[smem, smem, hbm, hbm],
        out_specs=[pl.BlockSpec(memory_space=pltpu.VMEM), hbm, hbm],
        scratch_shapes=[
            pltpu.VMEM((2, ROWS, WIDTH), jnp.bfloat16),
            block, block, block, block,
            pltpu.VMEM((2, ROWS, WIDTH), jnp.float32),
            pltpu.VMEM((2, ROWS, 128), jnp.float32),
            pltpu.SemaphoreType.DMA((2,)),
            pltpu.SemaphoreType.DMA((ROWS // TILE + 1,)),
            pltpu.SemaphoreType.DMA((CHUNKS,)),
            pltpu.SemaphoreType.DMA((CHUNKS,)),
            pltpu.SemaphoreType.DMA((CHUNKS,)),
            pltpu.SemaphoreType.DMA((CHUNKS,)),
            pltpu.SemaphoreType.DMA((CHUNKS,)),
            pltpu.SemaphoreType.DMA((CHUNKS,)),
            pltpu.SemaphoreType.DMA((2,)),
        ],
        compiler_params=pltpu.CompilerParams(
            collective_id=0, has_side_effects=True, vmem_limit_bytes=48 * 2**20
        ),
        cost_estimate=pl.CostEstimate(
            flops=24 * ROWS * ROWS * WIDTH, bytes_accessed=12 * ROWS * WIDTH, transcendentals=18 * ROWS * ROWS
        ),
    )(sharpness_multiplier, offset_shift, caption_embeds, picture_embeds)
    return loss.reshape(ROWS), image, text


def solution(mesh):
    in_specs = (P(("dp", "rep"), None), P(("dp", "rep"), None), P(), P())
    out_specs = (P(("dp", "rep")), P(("dp", "rep"), None), P(("dp", "rep"), None))
    return jax.shard_map(shards, mesh=mesh, in_specs=in_specs, out_specs=out_specs, check_vma=False)
```

time: 229 us -> 104 us (0.45)
  the two profiles are of different devices: /device:TPU:1 before, /device:TPU:29 now
where the time goes in v1:
time: 104 us
  Pallas kernels  92.4 us (89%)
  local copies, waits for them, and re-layouts  8.91 us (9%)
  between operations  1.94 us (2%)
    pallas_call x1, Pallas kernels, shards(): pl.pallas_call(kernel, out_shape=[jax.ShapeDtypeStruct((1, ROWS), jnp.flo...  92.4 us
    unnamed x8, local copies, waits for them, and re-layouts  8.91 us

profile of v1, /device:TPU:29, one launch (start us, length us, event | category | flops | bytes accessed | tf_op | source)
XLA Modules:
  0.0 103.8 jit_solution(4556623536756965764)
XLA Ops:
  1.9 0.0 copy-start
  1.9 1.5 %copy-done = bf16[768,1152]{1,0:T(8,128)(2,1)S(1)} copy-done((bf16[768,1152]{1,0:T(8,128)(2,1)S(1)}, bf16[768,1152]{1,0:T(8,128)(2,1)}, u32[]{:S(2)}) %copy-start) | copy-done | bytes 1769496
  3.4 0.0 copy-start.1
  3.4 1.5 %copy-done.1 = bf16[768,1152]{1,0:T(8,128)(2,1)S(1)} copy-done((bf16[768,1152]{1,0:T(8,128)(2,1)S(1)}, bf16[768,1152]{1,0:T(8,128)(2,1)}, u32[]{:S(2)}) %copy-start.1) | copy-done | bytes 1769496
  4.9 92.4 %shard_map.67 = (f32[1,768]{1,0:T(1,128)S(1)}, f32[768,1152]{1,0:T(8,128)}, f32[768,1152]{1,0:T(8,128)}) custom-call(f32[1]{0:T(128)S(6)} %copy.9.scale_ref, f32[1]{0:T(128)S(6)} %copy.10.shift_ref, bf16[768,1152]{1,0:T(8,128)(2,1)S(1)} %copy-done, bf16[768,1152]{1,0:T(8,128)(2,1)S(1)} %copy-done.1), custom_call_target="tpu_custom_call" | custom-call | flops 16307453952 | bytes 10616832 | tf_op jit(solution)/shard_map/pallas_call | solution.py:222
  97.2 0.6 reduce
  97.9 0.0 copy-start.2
  97.9 4.2 %copy.11 = f32[768,1152]{1,0:T(8,128)} copy(f32[768,1152]{1,0:T(8,128)} %get-tuple-element.13) | data formatting | bytes 7077888
  102.0 0.0 copy-done.2
  102.0 1.8 %copy.12 = f32[768,1152]{1,0:T(8,128)} copy(f32[768,1152]{1,0:T(8,128)S(1)} %copy-done.2) | data formatting | bytes 7077888
Async XLA Ops:
  1.9 1.5 %copy-start = (bf16[768,1152]{1,0:T(8,128)(2,1)S(1)}, bf16[768,1152]{1,0:T(8,128)(2,1)}, u32[]{:S(2)}) copy-start(bf16[768,1152]{1,0:T(8,128)(2,1)} %text_ref.1) | copy-start | bytes 5308420
  3.4 1.5 %copy-start.1 = (bf16[768,1152]{1,0:T(8,128)(2,1)S(1)}, bf16[768,1152]{1,0:T(8,128)(2,1)}, u32[]{:S(2)}) copy-start(bf16[768,1152]{1,0:T(8,128)(2,1)} %image_ref.1) | copy-start | bytes 5308420
  97.9 4.2 %copy-start.2 = (f32[768,1152]{1,0:T(8,128)S(1)}, f32[768,1152]{1,0:T(8,128)}, u32[]{:S(2)}) copy-start(f32[768,1152]{1,0:T(8,128)} %get-tuple-element.14) | copy-start | bytes 10616836

commit v2 on v1

v2 whole, which is shorter than its diff:
```python
import jax
import jax.numpy as jnp
from jax import lax
from jax.experimental import pallas as pl
from jax.experimental.pallas import tpu as pltpu
from jax.sharding import PartitionSpec as P

MESH = pl.DeviceIdType.MESH
N_REP = 4
DEVICES = 256
ROWS = 768
WIDTH = 1152
CHUNK = 128
CHUNKS = ROWS // CHUNK
TILE = 256
FAR_WINDOW = 3
NEAR_WINDOW = 2


def meet(near_or_far, block, scale, shift, tile, start=None):
    part = pl.ds(pl.multiple_of(jnp.int32(tile) * TILE, TILE), TILE)
    count = block.shape[0]
    logits = (
        lax.dot_general(
            near_or_far[part, :], block, (((1,), (1,)), ((), ())), preferred_element_type=jnp.float32
        )
        * scale
        + shift
    )
    decay = jnp.exp(-jnp.abs(logits))
    chance = jnp.where(logits >= 0, 1.0, decay) / (1.0 + decay)
    if start is not None:
        row = lax.broadcasted_iota(jnp.int32, (TILE, count), 0) + tile * TILE
        column = lax.broadcasted_iota(jnp.int32, (TILE, count), 1) + start
        same = row == column
        chance = chance - jnp.where(same, 1.0, 0.0)
        logits = jnp.where(same, -logits, logits)
    cost = jnp.maximum(logits, 0.0) + jnp.log1p(decay)
    total = cost[:, :128]
    for piece in range(1, count // 128):
        total = total + cost[:, piece * 128 : (piece + 1) * 128]
    change = jnp.dot(chance.astype(jnp.bfloat16), block, preferred_element_type=jnp.float32)
    return total, change


def kernel(
    scale_ref, shift_ref, text_ref, image_ref,
    own, got_near, grads, losses,
    got_far, beside, passed,
    load_sem, far_send, far_recv, near_send, near_recv, pass_send, pass_recv, beside_sem,
):
    dp, rep = lax.axis_index("dp"), lax.axis_index("rep")
    parity = lax.rem(rep, 2)
    me = dp * N_REP + rep

    def place(index):
        index = lax.rem(index + DEVICES, DEVICES)
        return (index // N_REP, lax.rem(index, N_REP))

    far_target = place(me - 2 + 4 * parity)
    near_target = place(me + 2 - 4 * parity)
    partner = (dp, rep + 1 - 2 * parity)

    loads = [
        pltpu.make_async_copy(text_ref, own.at[parity], load_sem.at[0]),
        pltpu.make_async_copy(image_ref, own.at[1 - parity], load_sem.at[1]),
    ]
    for load in loads:
        load.start()
    barrier = pltpu.get_barrier_semaphore()
    for target in (far_target, near_target, partner):
        pl.semaphore_signal(barrier, inc=1, device_id=target, device_id_type=MESH)

    scale = scale_ref[0]
    shift = shift_ref[0]

    def rows(chunk):
        return pl.ds(pl.multiple_of(chunk * CHUNK, CHUNK), CHUNK)

    def far_copy(chunk, source=image_ref):
        return pltpu.make_async_remote_copy(
            src_ref=source.at[rows(chunk)], dst_ref=got_far.at[rows(chunk)],
            send_sem=far_send.at[chunk], recv_sem=far_recv.at[chunk],
            device_id=far_target, device_id_type=MESH,
        )

    def near_copy(chunk, source=text_ref):
        return pltpu.make_async_remote_copy(
            src_ref=source.at[rows(chunk)], dst_ref=got_near.at[rows(chunk)],
            send_sem=near_send.at[chunk], recv_sem=near_recv.at[chunk],
            device_id=near_target, device_id_type=MESH,
        )

    def beside_copy(source=text_ref):
        return pltpu.make_async_remote_copy(
            src_ref=source, dst_ref=beside, send_sem=beside_sem.at[0], recv_sem=beside_sem.at[1],
            device_id=partner, device_id_type=MESH,
        )

    def pass_copy(chunk):
        return pltpu.make_async_remote_copy(
            src_ref=got_far.at[rows(chunk)], dst_ref=passed.at[rows(chunk)],
            send_sem=pass_send.at[chunk], recv_sem=pass_recv.at[chunk],
            device_id=partner, device_id_type=MESH,
        )

    def send(fars, nears, with_beside=False):
        for side, (far_source, near_source) in enumerate(((image_ref, text_ref), (text_ref, image_ref))):

            @pl.when(parity == side)
            def _():
                for step in range(max(len(fars), len(nears))):
                    if step < len(fars):
                        far_copy(fars[step], far_source).start()
                    if step < len(nears):
                        near_copy(nears[step], near_source).start()
                    if step == 0 and with_beside:
                        beside_copy(near_source).start()

    def gather(slot, other, start, count, diagonal=False, factor=None):
        block = other[pl.ds(start, count), :]

        def one(tile, carry):
            part = pl.ds(pl.multiple_of(tile * TILE, TILE), TILE)
            total, change = meet(own.at[slot], block, scale, shift, tile, start if diagonal else None)
            losses[slot, part, :] += total
            if factor is None:
                grads[slot, part, :] += change
            else:
                grads[slot, part, :] = (grads[slot, part, :] + change) * factor
            return carry

        lax.fori_loop(0, ROWS // TILE, one, 0)

    pl.semaphore_wait(barrier, 3)
    send(range(FAR_WINDOW), range(NEAR_WINDOW), True)
    grads[...] = jnp.zeros_like(grads)
    losses[...] = jnp.zeros_like(losses)
    for load in loads:
        load.wait()

    def local(step, carry):
        start = pl.multiple_of(step * TILE, TILE)
        gather(0, own.at[1], start, TILE, True)
        gather(1, own.at[0], start, TILE, True)
        return carry

    lax.fori_loop(0, ROWS // TILE, local, 0)
    beside_copy().wait()

    def inside(step, carry):
        gather(0, beside, pl.multiple_of(step * TILE, TILE), TILE)
        return carry

    lax.fori_loop(0, ROWS // TILE, inside, 0)

    def take_far(chunk):
        copy = far_copy(chunk)
        copy.wait_recv()
        pass_copy(chunk).start()
        copy.wait_send()

        @pl.when(chunk + FAR_WINDOW < CHUNKS)
        def _():
            send([chunk + FAR_WINDOW], [])

        factor = jnp.where(chunk == CHUNKS - 1, scale, 1.0)
        gather(0, got_far, pl.multiple_of(chunk * CHUNK, CHUNK), CHUNK, False, factor)

    def take_passed(chunk):
        pass_copy(chunk).wait()
        gather(1, passed, pl.multiple_of(chunk * CHUNK, CHUNK), CHUNK)

    def take_near(chunk):
        copy = near_copy(chunk)
        copy.wait_recv()
        copy.wait_send()

        @pl.when(chunk + NEAR_WINDOW < CHUNKS)
        def _():
            send([], [chunk + NEAR_WINDOW])

        @pl.when(chunk < CHUNKS - 1)
        def _():
            gather(1, got_near, pl.multiple_of(chunk * CHUNK, CHUNK), CHUNK)

    def across(chunk, carry):
        @pl.when(chunk >= 1)
        def _():
            take_passed(chunk - 1)

        @pl.when(chunk < CHUNKS)
        def _():
            take_far(chunk)

        @pl.when(chunk >= 1)
        def _():
            take_near(chunk - 1)

        return carry

    lax.fori_loop(0, CHUNKS + 1, across, 0)


def closing(scale_ref, shift_ref, own, got_near, grads, losses, loss_out, image_out, text_out, scaled, cost, sem):
    parity = lax.rem(lax.axis_index("rep"), 2)
    scale = scale_ref[0]
    shift = shift_ref[0]
    tiles = ROWS // TILE

    def store(source, output, tile, which):
        part = pl.ds(tile * TILE, TILE)
        return pltpu.make_async_copy(source.at[part], output.at[part], sem.at[which * tiles + tile])

    for side, output in enumerate((text_out, image_out)):

        @pl.when(parity == side)
        def _():
            for tile in range(tiles):
                store(grads.at[0], output, tile, 0).start()

    block = got_near[pl.ds(ROWS - CHUNK, CHUNK), :]
    for tile in range(tiles):
        part = pl.ds(tile * TILE, TILE)
        total, change = meet(own.at[1], block, scale, shift, tile)
        scaled[part, :] = (grads[1, part, :] + change) * scale

        for side, output in enumerate((image_out, text_out)):

            @pl.when(parity == side)
            def _():
                store(scaled, output, tile, 1).start()

        image_losses = jnp.where(parity == 0, losses[1, part, :] + total, losses[0, part, :])
        cost[part] = jnp.sum(image_losses.T, axis=0)
    loss_store = pltpu.make_async_copy(cost, loss_out, sem.at[2 * tiles])
    loss_store.start()
    for tile in range(tiles):
        store(grads.at[0], text_out, tile, 0).wait()
        store(scaled, image_out, tile, 1).wait()
    loss_store.wait()


def shards(picture_embeds, caption_embeds, sharpness_multiplier, offset_shift):
    smem = pl.BlockSpec(memory_space=pltpu.SMEM)
    vmem = pl.BlockSpec(memory_space=pltpu.VMEM)
    hbm = pl.BlockSpec(memory_space=pltpu.HBM)
    block = pltpu.VMEM((ROWS, WIDTH), jnp.bfloat16)
    chunk_sems = pltpu.SemaphoreType.DMA((CHUNKS,))
    kept = pl.pallas_call(
        kernel,
        out_shape=[
            pltpu.VMEM((2, ROWS, WIDTH), jnp.bfloat16),
            pltpu.VMEM((ROWS, WIDTH), jnp.bfloat16),
            pltpu.VMEM((2, ROWS, WIDTH), jnp.float32),
            pltpu.VMEM((2, ROWS, 128), jnp.float32),
        ],
        in_specs=[smem, smem, hbm, hbm],
        out_specs=[vmem] * 4,
        scratch_shapes=[
            block, block, block,
            pltpu.SemaphoreType.DMA((2,)),
            chunk_sems, chunk_sems, chunk_sems, chunk_sems, chunk_sems, chunk_sems,
            pltpu.SemaphoreType.DMA((2,)),
        ],
        compiler_params=pltpu.CompilerParams(
            collective_id=0, has_side_effects=True, vmem_limit_bytes=40 * 2**20
        ),
        cost_estimate=pl.CostEstimate(
            flops=24 * ROWS * ROWS * WIDTH, bytes_accessed=12 * ROWS * WIDTH, transcendentals=18 * ROWS * ROWS
        ),
    )(
        sharpness_multiplier,
        offset_shift,
        pltpu.with_memory_space_constraint(caption_embeds, pltpu.HBM),
        pltpu.with_memory_space_constraint(picture_embeds, pltpu.HBM),
    )
    kept = [pltpu.with_memory_space_constraint(value, pltpu.VMEM) for value in kept]
    return pl.pallas_call(
        closing,
        out_shape=[
            jax.ShapeDtypeStruct((ROWS,), jnp.float32),
            jax.ShapeDtypeStruct((ROWS, WIDTH), jnp.float32),
            jax.ShapeDtypeStruct((ROWS, WIDTH), jnp.float32),
        ],
        in_specs=[smem, smem, vmem, vmem, vmem, vmem],
        out_specs=[hbm, hbm, hbm],
        scratch_shapes=[
            pltpu.VMEM((ROWS, WIDTH), jnp.float32),
            pltpu.VMEM((ROWS,), jnp.float32),
            pltpu.SemaphoreType.DMA((2 * ROWS // TILE + 1,)),
        ],
        compiler_params=pltpu.CompilerParams(vmem_limit_bytes=40 * 2**20),
        cost_estimate=pl.CostEstimate(
            flops=4 * CHUNK * ROWS * WIDTH, bytes_accessed=8 * ROWS * WIDTH, transcendentals=3 * CHUNK * ROWS
        ),
    )(sharpness_multiplier, offset_shift, *kept)


def solution(mesh):
    in_specs = (P(("dp", "rep"), None), P(("dp", "rep"), None), P(), P())
    out_specs = (P(("dp", "rep")), P(("dp", "rep"), None), P(("dp", "rep"), None))
    return jax.shard_map(shards, mesh=mesh, in_specs=in_specs, out_specs=out_specs, check_vma=False)
```

time: 104 us -> 94 us (0.904)
  the two profiles are of different devices: /device:TPU:29 before, /device:TPU:2 now
where the time goes in v2:
time: 94 us; the launch traced here: 93.9 us
  Pallas kernels  92 us (98%)
  between operations  1.93 us (2%)
    pallas_call x1, Pallas kernels, shards(): pl.pallas_call(kernel, out_shape=[pltpu.VMEM((2, ROWS, WIDTH), jnp.bfloat...  88.8 us
    pallas_call x1, Pallas kernels, shards(): pl.pallas_call(closing, out_shape=[jax.ShapeDtypeStruct((ROWS,), jnp.floa...  3.22 us

profile of v2, /device:TPU:2, one launch (start us, length us, event | category | flops | bytes accessed | tf_op | source)
XLA Modules:
  0.0 93.9 jit_solution(4407234106228342658)
XLA Ops:
  1.9 88.8 %shard_map.67 = (bf16[2,768,1152]{2,1,0:T(8,128)(2,1)S(1)}, bf16[768,1152]{1,0:T(8,128)(2,1)S(1)}, f32[2,768,1152]{2,1,0:T(8,128)S(1)}, f32[2,768,128]{2,1,0:T(8,128)S(1)}) custom-call(f32[1]{0:T(128)S(6)} %copy.7.scale_ref, f32[1]{0:T(128)S(6)} %copy.8.shift_ref, bf16[768,1152]{1,0:T(8,128)(2,1)} %text_ref.1, bf16[768,1152]{1,0:T(8,128)(2,1)} %image_ref.1), custom_call_target="tpu_custom_call" | custom-call | flops 16307453952 | bytes 10616832 | tf_op jit(solution)/shard_map/pallas_call | solution.py:250
  90.7 3.2 %shard_map.68 = (f32[768]{0:T(1024)}, f32[768,1152]{1,0:T(8,128)}, f32[768,1152]{1,0:T(8,128)}) custom-call(f32[1]{0:T(128)S(6)} %copy.7.scale_ref, f32[1]{0:T(128)S(6)} %copy.8.shift_ref, bf16[2,768,1152]{2,1,0:T(8,128)(2,1)S(1)} %get-tuple-element.7.own, bf16[768,1152]{1,0:T(8,128)(2,1)S(1)} %get-tuple-element.8.got_near, ...), custom_call_target="tpu_custom_call" | custom-call | flops 452984832 | bytes 7077888 | tf_op jit(solution)/shard_map/pallas_call | solution.py:279

commit v3 on v2

--- a/solution.py
+++ b/solution.py
@@ -13,8 +13,7 @@
 CHUNK = 128
 CHUNKS = ROWS // CHUNK
 TILE = 256
-FAR_WINDOW = 3
-NEAR_WINDOW = 2
+WINDOW = 2
 
 
 def meet(near_or_far, block, scale, shift, tile, start=None):
@@ -28,15 +27,19 @@
         + shift
     )
     decay = jnp.exp(-jnp.abs(logits))
-    chance = jnp.where(logits >= 0, 1.0, decay) / (1.0 + decay)
+    above = 1.0 + decay
+    inverse = pl.reciprocal(above, approx=True)
+    inverse = inverse * (2.0 - above * inverse)
+    chance = jnp.where(logits >= 0, inverse, decay * inverse)
+    log_above = jnp.log(above) + (decay - (above - 1.0)) * inverse
     if start is not None:
         row = lax.broadcasted_iota(jnp.int32, (TILE, count), 0) + tile * TILE
         column = lax.broadcasted_iota(jnp.int32, (TILE, count), 1) + start
         same = row == column
         chance = chance - jnp.where(same, 1.0, 0.0)
         logits = jnp.where(same, -logits, logits)
-    cost = jnp.maximum(logits, 0.0) + jnp.log1p(decay)
-    total = cost[:, :128]
+    cost = jnp.maximum(logits, 0.0) + log_above
+    total = cost[:, : min(count, 128)]
     for piece in range(1, count // 128):
         total = total + cost[:, piece * 128 : (piece + 1) * 128]
     change = jnp.dot(chance.astype(jnp.bfloat16), block, preferred_element_type=jnp.float32)
@@ -123,83 +126,70 @@
         def one(tile, carry):
             part = pl.ds(pl.multiple_of(tile * TILE, TILE), TILE)
             total, change = meet(own.at[slot], block, scale, shift, tile, start if diagonal else None)
-            losses[slot, part, :] += total
+            losses[slot, part, : total.shape[1]] += total
             if factor is None:
                 grads[slot, part, :] += change
             else:
                 grads[slot, part, :] = (grads[slot, part, :] + change) * factor
             return carry
 
-        lax.fori_loop(0, ROWS // TILE, one, 0)
+        for tile in range(ROWS // TILE):
+            one(tile, 0)
 
     pl.semaphore_wait(barrier, 3)
-    send(range(FAR_WINDOW), range(NEAR_WINDOW), True)
+    send(range(WINDOW), [], True)
     grads[...] = jnp.zeros_like(grads)
     losses[...] = jnp.zeros_like(losses)
     for load in loads:
         load.wait()
+    send([], range(WINDOW))
 
     def local(step, carry):
-        start = pl.multiple_of(step * TILE, TILE)
-        gather(0, own.at[1], start, TILE, True)
-        gather(1, own.at[0], start, TILE, True)
+        slot = lax.rem(step, 2)
+        gather(slot, own.at[1 - slot], pl.multiple_of(step // 2 * TILE, TILE), TILE, True)
         return carry
 
-    lax.fori_loop(0, ROWS // TILE, local, 0)
+    lax.fori_loop(0, 2 * ROWS // TILE, local, 0)
     beside_copy().wait()
 
     def inside(step, carry):
-        gather(0, beside, pl.multiple_of(step * TILE, TILE), TILE)
+        gather(0, beside, pl.multiple_of(step * TILE, TILE), 256)
         return carry
 
     lax.fori_loop(0, ROWS // TILE, inside, 0)
 
-    def take_far(chunk):
-        copy = far_copy(chunk)
-        copy.wait_recv()
+    def refill_far(chunk):
+        far_copy(chunk).wait_send()
+
+        @pl.when(chunk + WINDOW < CHUNKS)
+        def _():
+            send([chunk + WINDOW], [])
+
+    def refill_near(chunk):
+        near_copy(chunk).wait_send()
+
+        @pl.when(chunk + WINDOW < CHUNKS)
+        def _():
+            send([], [chunk + WINDOW])
+
+    def across(chunk, carry):
+        start = pl.multiple_of(chunk * CHUNK, CHUNK)
+        refill_far(chunk)
+        far_copy(chunk).wait_recv()
         pass_copy(chunk).start()
-        copy.wait_send()
-
-        @pl.when(chunk + FAR_WINDOW < CHUNKS)
-        def _():
-            send([chunk + FAR_WINDOW], [])
-
-        factor = jnp.where(chunk == CHUNKS - 1, scale, 1.0)
-        gather(0, got_far, pl.multiple_of(chunk * CHUNK, CHUNK), CHUNK, False, factor)
-
-    def take_passed(chunk):
+        gather(0, got_far, start, CHUNK, False, jnp.where(chunk == CHUNKS - 1, scale, 1.0))
         pass_copy(chunk).wait()
-        gather(1, passed, pl.multiple_of(chunk * CHUNK, CHUNK), CHUNK)
-
-    def take_near(chunk):
-        copy = near_copy(chunk)
-        copy.wait_recv()
-        copy.wait_send()
-
-        @pl.when(chunk + NEAR_WINDOW < CHUNKS)
-        def _():
-            send([], [chunk + NEAR_WINDOW])
+        gather(1, passed, start, CHUNK)
+        refill_near(chunk)
+        near_copy(chunk).wait_recv()
 
         @pl.when(chunk < CHUNKS - 1)
         def _():
-            gather(1, got_near, pl.multiple_of(chunk * CHUNK, CHUNK), CHUNK)
-
-    def across(chunk, carry):
-        @pl.when(chunk >= 1)
-        def _():
-            take_passed(chunk - 1)
-
-        @pl.when(chunk < CHUNKS)
-        def _():
-            take_far(chunk)
-
-        @pl.when(chunk >= 1)
-        def _():
-            take_near(chunk - 1)
+            gather(1, got_near, start, CHUNK)
 
         return carry
 
-    lax.fori_loop(0, CHUNKS + 1, across, 0)
+    lax.fori_loop(0, CHUNKS, across, 0)
 
 
 def closing(scale_ref, shift_ref, own, got_near, grads, losses, loss_out, image_out, text_out, scaled, cost, sem):

time: 94 us -> 91.4 us (0.972)
  the two profiles are of different devices: /device:TPU:2 before, /device:TPU:1 now
where the time goes in v3:
time: 91.4 us; the launch traced here: 91.2 us
  Pallas kernels  89.3 us (98%)
  between operations  1.93 us (2%)
    pallas_call x1, Pallas kernels, shards(): pl.pallas_call(kernel, out_shape=[pltpu.VMEM((2, ROWS, WIDTH), jnp.bfloat...  86.1 us
    pallas_call x1, Pallas kernels, shards(): pl.pallas_call(closing, out_shape=[jax.ShapeDtypeStruct((ROWS,), jnp.floa...  3.22 us

profile of v3, /device:TPU:1, one launch (start us, length us, event | category | flops | bytes accessed | tf_op | source)
XLA Modules:
  0.0 91.2 jit_solution(1603947996805014993)
XLA Ops:
  1.9 86.1 %shard_map.67 = (bf16[2,768,1152]{2,1,0:T(8,128)(2,1)S(1)}, bf16[768,1152]{1,0:T(8,128)(2,1)S(1)}, f32[2,768,1152]{2,1,0:T(8,128)S(1)}, f32[2,768,128]{2,1,0:T(8,128)S(1)}) custom-call(f32[1]{0:T(128)S(6)} %copy.7.scale_ref, f32[1]{0:T(128)S(6)} %copy.8.shift_ref, bf16[768,1152]{1,0:T(8,128)(2,1)} %text_ref.1, bf16[768,1152]{1,0:T(8,128)(2,1)} %image_ref.1), custom_call_target="tpu_custom_call" | custom-call | flops 16307453952 | bytes 10616832 | tf_op jit(solution)/shard_map/pallas_call | solution.py:240
  88.0 3.2 %shard_map.68 = (f32[768]{0:T(1024)}, f32[768,1152]{1,0:T(8,128)}, f32[768,1152]{1,0:T(8,128)}) custom-call(f32[1]{0:T(128)S(6)} %copy.7.scale_ref, f32[1]{0:T(128)S(6)} %copy.8.shift_ref, bf16[2,768,1152]{2,1,0:T(8,128)(2,1)S(1)} %get-tuple-element.7.own, bf16[768,1152]{1,0:T(8,128)(2,1)S(1)} %get-tuple-element.8.got_near, ...), custom_call_target="tpu_custom_call" | custom-call | flops 452984832 | bytes 7077888 | tf_op jit(solution)/shard_map/pallas_call | solution.py:269

commit v4 on v3

--- a/solution.py
+++ b/solution.py
@@ -48,8 +48,8 @@
 
 def kernel(
     scale_ref, shift_ref, text_ref, image_ref,
-    own, got_near, grads, losses,
-    got_far, beside, passed,
+    own, met, grads, losses,
+    got_far, beside,
     load_sem, far_send, far_recv, near_send, near_recv, pass_send, pass_recv, beside_sem,
 ):
     dp, rep = lax.axis_index("dp"), lax.axis_index("rep")
@@ -89,7 +89,7 @@
 
     def near_copy(chunk, source=text_ref):
         return pltpu.make_async_remote_copy(
-            src_ref=source.at[rows(chunk)], dst_ref=got_near.at[rows(chunk)],
+            src_ref=source.at[rows(chunk)], dst_ref=met.at[rows(2 * chunk + 1)],
             send_sem=near_send.at[chunk], recv_sem=near_recv.at[chunk],
             device_id=near_target, device_id_type=MESH,
         )
@@ -102,7 +102,7 @@
 
     def pass_copy(chunk):
         return pltpu.make_async_remote_copy(
-            src_ref=got_far.at[rows(chunk)], dst_ref=passed.at[rows(chunk)],
+            src_ref=got_far.at[rows(chunk)], dst_ref=met.at[rows(2 * chunk)],
             send_sem=pass_send.at[chunk], recv_sem=pass_recv.at[chunk],
             device_id=partner, device_id_type=MESH,
         )
@@ -173,26 +173,25 @@
             send([], [chunk + WINDOW])
 
     def across(chunk, carry):
-        start = pl.multiple_of(chunk * CHUNK, CHUNK)
         refill_far(chunk)
         far_copy(chunk).wait_recv()
         pass_copy(chunk).start()
-        gather(0, got_far, start, CHUNK, False, jnp.where(chunk == CHUNKS - 1, scale, 1.0))
-        pass_copy(chunk).wait()
-        gather(1, passed, start, CHUNK)
+        factor = jnp.where(chunk == CHUNKS - 1, scale, 1.0)
+        gather(0, got_far, pl.multiple_of(chunk * CHUNK, CHUNK), CHUNK, False, factor)
         refill_near(chunk)
         near_copy(chunk).wait_recv()
+        pass_copy(chunk).wait()
 
         @pl.when(chunk < CHUNKS - 1)
         def _():
-            gather(1, got_near, start, CHUNK)
+            gather(1, met, pl.multiple_of(2 * chunk * CHUNK, CHUNK), 2 * CHUNK)
 
         return carry
 
     lax.fori_loop(0, CHUNKS, across, 0)
 
 
-def closing(scale_ref, shift_ref, own, got_near, grads, losses, loss_out, image_out, text_out, scaled, cost, sem):
+def closing(scale_ref, shift_ref, own, met, grads, losses, loss_out, image_out, text_out, scaled, cost, sem):
     parity = lax.rem(lax.axis_index("rep"), 2)
     scale = scale_ref[0]
     shift = shift_ref[0]
@@ -209,7 +208,7 @@
             for tile in range(tiles):
                 store(grads.at[0], output, tile, 0).start()
 
-    block = got_near[pl.ds(ROWS - CHUNK, CHUNK), :]
+    block = met[pl.ds(2 * (ROWS - CHUNK), 2 * CHUNK), :]
     for tile in range(tiles):
         part = pl.ds(tile * TILE, TILE)
         total, change = meet(own.at[1], block, scale, shift, tile)
@@ -241,14 +240,14 @@
         kernel,
         out_shape=[
             pltpu.VMEM((2, ROWS, WIDTH), jnp.bfloat16),
-            pltpu.VMEM((ROWS, WIDTH), jnp.bfloat16),
+            pltpu.VMEM((2 * ROWS, WIDTH), jnp.bfloat16),
             pltpu.VMEM((2, ROWS, WIDTH), jnp.float32),
             pltpu.VMEM((2, ROWS, 128), jnp.float32),
         ],
         in_specs=[smem, smem, hbm, hbm],
         out_specs=[vmem] * 4,
         scratch_shapes=[
-            block, block, block,
+            block, block,
             pltpu.SemaphoreType.DMA((2,)),
             chunk_sems, chunk_sems, chunk_sems, chunk_sems, chunk_sems, chunk_sems,
             pltpu.SemaphoreType.DMA((2,)),
@@ -282,7 +281,7 @@
         ],
         compiler_params=pltpu.CompilerParams(vmem_limit_bytes=40 * 2**20),
         cost_estimate=pl.CostEstimate(
-            flops=4 * CHUNK * ROWS * WIDTH, bytes_accessed=8 * ROWS * WIDTH, transcendentals=3 * CHUNK * ROWS
+            flops=8 * CHUNK * ROWS * WIDTH, bytes_accessed=8 * ROWS * WIDTH, transcendentals=6 * CHUNK * ROWS
         ),
     )(sharpness_multiplier, offset_shift, *kept)
 

time: 91.4 us -> 89.9 us (0.984)
  Pallas kernels: 89.3 us -> 87.8 us
    pallas_call x1, Pallas kernels: 86.1 us -> 84.3 us  [shards(): pl.pallas_call(kernel, out_shape=[pltpu.VMEM((2, ROWS, WIDTH), jnp.bfloat...]
where the time goes in v4:
time: 89.9 us; the launch traced here: 89.7 us
  Pallas kernels  87.8 us (98%)
  between operations  1.93 us (2%)
    pallas_call x1, Pallas kernels, shards(): pl.pallas_call(kernel, out_shape=[pltpu.VMEM((2, ROWS, WIDTH), jnp.bfloat...  84.3 us
    pallas_call x1, Pallas kernels, shards(): pl.pallas_call(closing, out_shape=[jax.ShapeDtypeStruct((ROWS,), jnp.floa...  3.47 us

profile of v4, /device:TPU:1, one launch (start us, length us, event | category | flops | bytes accessed | tf_op | source)
XLA Modules:
  0.0 89.7 jit_solution(10280866682286711727)
XLA Ops:
  1.9 84.3 %shard_map.67 = (bf16[2,768,1152]{2,1,0:T(8,128)(2,1)S(1)}, bf16[1536,1152]{1,0:T(8,128)(2,1)S(1)}, f32[2,768,1152]{2,1,0:T(8,128)S(1)}, f32[2,768,128]{2,1,0:T(8,128)S(1)}) custom-call(f32[1]{0:T(128)S(6)} %copy.7.scale_ref, f32[1]{0:T(128)S(6)} %copy.8.shift_ref, bf16[768,1152]{1,0:T(8,128)(2,1)} %text_ref.1, bf16[768,1152]{1,0:T(8,128)(2,1)} %image_ref.1), custom_call_target="tpu_custom_call" | custom-call | flops 16307453952 | bytes 10616832 | tf_op jit(solution)/shard_map/pallas_call | solution.py:239
  86.3 3.5 %shard_map.68 = (f32[768]{0:T(1024)}, f32[768,1152]{1,0:T(8,128)}, f32[768,1152]{1,0:T(8,128)}) custom-call(f32[1]{0:T(128)S(6)} %copy.7.scale_ref, f32[1]{0:T(128)S(6)} %copy.8.shift_ref, bf16[2,768,1152]{2,1,0:T(8,128)(2,1)S(1)} %get-tuple-element.7.own, bf16[1536,1152]{1,0:T(8,128)(2,1)S(1)} %get-tuple-element.8.met, ...), custom_call_target="tpu_custom_call" | custom-call | flops 905969664 | bytes 7077888 | tf_op jit(solution)/shard_map/pallas_call | solution.py:268

commit v5 on v4

--- a/solution.py
+++ b/solution.py
@@ -142,9 +142,12 @@
     losses[...] = jnp.zeros_like(losses)
     for load in loads:
         load.wait()
-    send([], range(WINDOW))
 
     def local(step, carry):
+        @pl.when(step == 1)
+        def _():
+            send([], range(WINDOW))
+
         slot = lax.rem(step, 2)
         gather(slot, own.at[1 - slot], pl.multiple_of(step // 2 * TILE, TILE), TILE, True)
         return carry

time: 89.9 us -> 90.5 us (level)
  no operation moved by 1% of the time
where the time goes in v5:
time: 90.5 us; the launch traced here: 90.3 us
  Pallas kernels  88.4 us (98%)
  between operations  1.93 us (2%)
    pallas_call x1, Pallas kernels, shards(): pl.pallas_call(kernel, out_shape=[pltpu.VMEM((2, ROWS, WIDTH), jnp.bfloat...  84.9 us
    pallas_call x1, Pallas kernels, shards(): pl.pallas_call(closing, out_shape=[jax.ShapeDtypeStruct((ROWS,), jnp.floa...  3.47 us

profile of v5, /device:TPU:1, one launch (start us, length us, event | category | flops | bytes accessed | tf_op | source)
XLA Modules:
  0.0 90.3 jit_solution(14919404391065128543)
XLA Ops:
  1.9 84.9 %shard_map.67 = (bf16[2,768,1152]{2,1,0:T(8,128)(2,1)S(1)}, bf16[1536,1152]{1,0:T(8,128)(2,1)S(1)}, f32[2,768,1152]{2,1,0:T(8,128)S(1)}, f32[2,768,128]{2,1,0:T(8,128)S(1)}) custom-call(f32[1]{0:T(128)S(6)} %copy.7.scale_ref, f32[1]{0:T(128)S(6)} %copy.8.shift_ref, bf16[768,1152]{1,0:T(8,128)(2,1)} %text_ref.1, bf16[768,1152]{1,0:T(8,128)(2,1)} %image_ref.1), custom_call_target="tpu_custom_call" | custom-call | flops 16307453952 | bytes 10616832 | tf_op jit(solution)/shard_map/pallas_call | solution.py:242
  86.9 3.5 %shard_map.68 = (f32[768]{0:T(1024)}, f32[768,1152]{1,0:T(8,128)}, f32[768,1152]{1,0:T(8,128)}) custom-call(f32[1]{0:T(128)S(6)} %copy.7.scale_ref, f32[1]{0:T(128)S(6)} %copy.8.shift_ref, bf16[2,768,1152]{2,1,0:T(8,128)(2,1)S(1)} %get-tuple-element.7.own, bf16[1536,1152]{1,0:T(8,128)(2,1)S(1)} %get-tuple-element.8.met, ...), custom_call_target="tpu_custom_call" | custom-call | flops 905969664 | bytes 7077888 | tf_op jit(solution)/shard_map/pallas_call | solution.py:271
